TPU v7x, 128 devices: a whole 4x4x4 slice. The times are simulated.
128 devices in a mesh: level: 4 (over x), grp: 32 (over z, y, core).
Axes of the slice: x: 4, y: 4, z: 4, core: 2. Of those that a mesh axis runs over, the one named last changes fastest.
Arguments:
- x_old: bfloat16 [4, 512, 16, 128], P('level', 'grp'), may hold values from -6 to 6
- rhs: float32 [4, 512, 16, 128], P('level', 'grp'), may hold values from -6 to 6
- down_tiles: bfloat16 [4, 512, 6, 128, 128], P('level', 'grp'), may hold values from -0.4375 to 0.4375
- level_tiles: bfloat16 [4, 512, 6, 128, 128], P('level', 'grp'), may hold values from -0.1875 to 0.1875
- up_tiles: bfloat16 [4, 512, 6, 128, 128], P('level', 'grp'), may hold values from -0.1875 to 0.1875
- inverses: float32 [4, 512, 128, 128], P('level', 'grp'), as said below
- tile_cols: int32 [4, 512, 3, 6], P('level', 'grp'), may hold values from 0 to 511
- tile_counts: int32 [4, 512, 3], P('level', 'grp'), may hold values from 1 to 6, as said below
Outputs:
- solution: float32 [4, 512, 16, 128], P('level', 'grp')
Inputs may be any that keep to these rules, and one draw needn't show every extreme that they name: `tile_counts`: slots at or beyond a block row's count are to be ignored; every level has a block row with 6 live slots in every band. `inverses`: each inverse is an arbitrary dense matrix given in full.
All inputs are finite; a program needn't handle non-finite values.
Results may differ from a plain program's by a relative error of at most 0.0015.
Values may be sent and summed in bfloat16 or wider, within the bound.
A program may use at most 64 MiB of HBM per device.

v0:
```python
import jax
import jax.numpy as jnp
from jax import lax
from jax.sharding import PartitionSpec as P


def from_behind(value, axis, by):
    length = lax.axis_size(axis)
    pairs = [(i, i + by) for i in range(length) if 0 <= i + by < length]
    return lax.ppermute(value, axis, pairs)


def band_term(tiles, cols, counts, source):
    pieces = source[cols]
    slots = jnp.arange(cols.shape[1], dtype=jnp.int32)
    live = slots[None, :] < counts[:, None]
    pieces = jnp.where(live[:, :, None, None], pieces, jnp.zeros((), pieces.dtype))
    return jnp.einsum("bkrc,bkcq->brq", pieces, tiles, preferred_element_type=jnp.float32)


def solve_blocks(resid, inverse):
    return jnp.einsum(
        "brc,bcq->brq",
        resid,
        inverse,
        precision=lax.Precision.HIGHEST,
        preferred_element_type=jnp.float32,
    )


def shards(x_old, rhs, down_tiles, level_tiles, up_tiles, inverses, tile_cols, tile_counts):
    own = x_old[0]
    whole = lax.all_gather(own, "grp", axis=0, tiled=True)
    above = from_behind(whole, "level", -1)
    cols = tile_cols[0]
    counts = tile_counts[0]
    base = rhs[0] - band_term(level_tiles[0], cols[:, 1], counts[:, 1], whole)
    base = base - band_term(up_tiles[0], cols[:, 2], counts[:, 2], above)
    inverse = inverses[0]
    down_here = down_tiles[0]
    first = solve_blocks(base, inverse)

    def level_turn(turn, current):
        outgoing = current.astype(jnp.bfloat16)
        gathered = lax.all_gather(outgoing, "grp", axis=0, tiled=True)
        panel = from_behind(gathered, "level", 1)
        resid = base - band_term(down_here, cols[:, 0], counts[:, 0], panel)
        return solve_blocks(resid, inverse)

    final = lax.fori_loop(1, lax.axis_size("level"), level_turn, first)
    return final[None]


def solution(mesh):
    return jax.shard_map(
        shards,
        mesh=mesh,
        in_specs=(
            P("level", "grp", None, None),
            P("level", "grp", None, None),
            P("level", "grp", None, None, None),
            P("level", "grp", None, None, None),
            P("level", "grp", None, None, None),
            P("level", "grp", None, None),
            P("level", "grp", None, None),
            P("level", "grp", None),
        ),
        out_specs=P("level", "grp", None, None),
        check_vma=False,
    )
```

profile of v0, /device:TPU:2, one launch (start us, length us, event | category | flops | bytes accessed | tf_op | source)
XLA Modules:
  0.0 425.3 jit_solution(5996172280538096552)
XLA Ops:
  7.3 48.8 %all-gather.4.cloned.1.call-done = bf16[1,512,16,128]{3,2,0,1:T(8,128)(2,1)} async-done(((bf16[1,16,16,128]{3,2,0,1:T(8,128)(2,1)}), bf16[1,512,16,128]{3,2,0,1:T(8,128)(2,1)}) %all-gather.4.cloned.1.call-update) | async-done | bytes 2097168 | tf_op jit(solution)/shard_map/all_gather | solution.py:33
  56.0 2.5 collective-permute-start.1
  58.5 1.3 copy.28
  59.8 0.8 compare_select_fusion.1
  62.1 2.3 gather_fusion.1
  64.3 2.1 fusion.18
  66.5 39.5 %collective-permute-done.1 = bf16[512,16,128]{2,1,0:T(8,128)(2,1)} collective-permute-done((bf16[512,16,128]{2,1,0:T(8,128)(2,1)}, bf16[512,16,128]{2,1,0:T(8,128)(2,1)}, u32[]{:S(2)}, u32[]{:S(2)}) %collective-permute-start.1) | collective-permute-done | bytes 2097184 | tf_op jit(solution)/shard_map/ppermute | solution.py:10
  106.0 2.3 gather_fusion.2
  108.3 2.5 fusion.15
  110.9 1.0 fusion.27
  111.8 306.3 %while.10 = (s32[]{:T(128)}, f32[16,16,128]{2,1,0:T(8,128)S(1)}, s32[16,3]{0,1:T(4,128)}, s32[16,3,6]{0,1,2:T(4,128)}, bf16[16,6,128,128]{3,2,1,0:T(8,128)(2,1)}...) while((s32[]{:T(128)}, f32[16,16,128]{2,1,0:T(8,128)S(1)}, s32[16,3]{0,1:T(4,128)}, ...), condition=%wide.region_1.2_spmd, body=%wide.region_0.1_spmd.sunk | while | flops 100926848 | bytes 25173568 | solution.py:50
  112.6 45.6 %all-gather.6.cloned.1.call-done = bf16[512,16,128]{2,1,0:T(8,128)(2,1)} async-done(((bf16[16,16,128]{2,1,0:T(8,128)(2,1)}), bf16[512,16,128]{2,1,0:T(8,128)(2,1)}) %all-gather.6.cloned.1.call-update) | async-done | bytes 2097168 | tf_op jit(solution)/shard_map/while/body/eval_jaxpr/all_gather | solution.py:45
  158.2 3.4 collective-permute-start
  161.6 0.7 compare_select_fusion.4
  163.2 45.0 %collective-permute-done = bf16[512,16,128]{2,1,0:T(8,128)(2,1)} collective-permute-done((bf16[512,16,128]{2,1,0:T(8,128)(2,1)}, bf16[512,16,128]{2,1,0:T(8,128)(2,1)}, u32[]{:S(2)}, u32[]{:S(2)}) %collective-permute-start) | collective-permute-done | bytes 2097184 | tf_op jit(solution)/shard_map/while/body/eval_jaxpr/ppermute | solution.py:10
  208.2 2.3 gather_fusion
  210.5 2.5 fusion.46
  213.1 1.0 fusion.47
  214.8 45.6 %all-gather.6.cloned.1.call-done = bf16[512,16,128]{2,1,0:T(8,128)(2,1)} async-done(((bf16[16,16,128]{2,1,0:T(8,128)(2,1)}), bf16[512,16,128]{2,1,0:T(8,128)(2,1)}) %all-gather.6.cloned.1.call-update) | async-done | bytes 2097168 | tf_op jit(solution)/shard_map/while/body/eval_jaxpr/all_gather | solution.py:45
  260.4 3.4 collective-permute-start
  263.8 0.7 compare_select_fusion.4
  265.4 45.0 %collective-permute-done = bf16[512,16,128]{2,1,0:T(8,128)(2,1)} collective-permute-done((bf16[512,16,128]{2,1,0:T(8,128)(2,1)}, bf16[512,16,128]{2,1,0:T(8,128)(2,1)}, u32[]{:S(2)}, u32[]{:S(2)}) %collective-permute-start) | collective-permute-done | bytes 2097184 | tf_op jit(solution)/shard_map/while/body/eval_jaxpr/ppermute | solution.py:10
  310.4 2.3 gather_fusion
  312.7 2.5 fusion.46
  315.2 1.0 fusion.47
  316.9 45.4 %all-gather.6.cloned.1.call-done = bf16[512,16,128]{2,1,0:T(8,128)(2,1)} async-done(((bf16[16,16,128]{2,1,0:T(8,128)(2,1)}), bf16[512,16,128]{2,1,0:T(8,128)(2,1)}) %all-gather.6.cloned.1.call-update) | async-done | bytes 2097168 | tf_op jit(solution)/shard_map/while/body/eval_jaxpr/all_gather | solution.py:45
  362.3 3.4 collective-permute-start
  365.7 0.7 compare_select_fusion.4
  367.3 45.0 %collective-permute-done = bf16[512,16,128]{2,1,0:T(8,128)(2,1)} collective-permute-done((bf16[512,16,128]{2,1,0:T(8,128)(2,1)}, bf16[512,16,128]{2,1,0:T(8,128)(2,1)}, u32[]{:S(2)}, u32[]{:S(2)}) %collective-permute-start) | collective-permute-done | bytes 2097184 | tf_op jit(solution)/shard_map/while/body/eval_jaxpr/ppermute | solution.py:10
  412.3 2.3 gather_fusion
  414.6 2.5 fusion.46
  417.1 1.0 fusion.47
  (51 shorter events, 7.8 us)
Async XLA Ops:
  6.5 57.8 %copy-start = (bf16[1,16,6,128,128]{4,3,2,1,0:T(8,128)(2,1)S(1)}, bf16[1,16,6,128,128]{4,3,2,1,0:T(8,128)(2,1)}, u32[]{:S(2)}) copy-start(bf16[1,16,6,128,128]{4,3,2,1,0:T(8,128)(2,1)} %param.13) | copy-start | bytes 9437188
  6.5 49.5 %all-gather.4.cloned.1.call-start = ((), (), s32[]{:S(2)}) async-start(), calls=%async_computation | async-start | bytes 2162688 | tf_op jit(solution)/shard_map/all_gather | solution.py:33
  56.0 50.0 %collective-permute-start.1 = (bf16[512,16,128]{2,1,0:T(8,128)(2,1)}, bf16[512,16,128]{2,1,0:T(8,128)(2,1)}, u32[]{:S(2)}, u32[]{:S(2)}) collective-permute-start(bf16[512,16,128]{2,1,0:T(8,128)(2,1)} %bitcast.92), channel_id=1, source_target_pairs={{32,0},{64,32},{96,64},{33,1},{65,33},{97,65},{34,2},{66,34},{98,6... | collective-permute-start | bytes 6291464 | tf_op jit(solution)/shard_map/ppermute | solution.py:10
  61.4 0.6 copy-start.5
  108.3 2.6 copy-start.1
  110.8 1.0 copy-start.3
  111.8 46.4 %all-gather.6.cloned.1.call-start = ((), (), s32[]{:S(2)}) async-start(), calls=%async_computation.1 | async-start | bytes 2162688 | tf_op jit(solution)/shard_map/while/body/eval_jaxpr/all_gather | solution.py:45
  158.2 50.0 %collective-permute-start = (bf16[512,16,128]{2,1,0:T(8,128)(2,1)}, bf16[512,16,128]{2,1,0:T(8,128)(2,1)}, u32[]{:S(2)}, u32[]{:S(2)}) collective-permute-start(bf16[512,16,128]{2,1,0:T(8,128)(2,1)} %all-gather.6.cloned.1.call-done), channel_id=1, source_target_pairs={{0,32},{32,64},{64,96},{1,33},{33,65},{65,97},{2,34},{34,66},{66,9... | collective-permute-start | bytes 6291464 | tf_op jit(solution)/shard_map/while/body/eval_jaxpr/ppermute | solution.py:10
  210.5 2.6 copy-start.2
  214.0 46.4 %all-gather.6.cloned.1.call-start = ((), (), s32[]{:S(2)}) async-start(), calls=%async_computation.1 | async-start | bytes 2162688 | tf_op jit(solution)/shard_map/while/body/eval_jaxpr/all_gather | solution.py:45
  260.4 50.0 %collective-permute-start = (bf16[512,16,128]{2,1,0:T(8,128)(2,1)}, bf16[512,16,128]{2,1,0:T(8,128)(2,1)}, u32[]{:S(2)}, u32[]{:S(2)}) collective-permute-start(bf16[512,16,128]{2,1,0:T(8,128)(2,1)} %all-gather.6.cloned.1.call-done), channel_id=1, source_target_pairs={{0,32},{32,64},{64,96},{1,33},{33,65},{65,97},{2,34},{34,66},{66,9... | collective-permute-start | bytes 6291464 | tf_op jit(solution)/shard_map/while/body/eval_jaxpr/ppermute | solution.py:10
  312.7 2.6 copy-start.2
  316.2 46.1 %all-gather.6.cloned.1.call-start = ((), (), s32[]{:S(2)}) async-start(), calls=%async_computation.1 | async-start | bytes 2162688 | tf_op jit(solution)/shard_map/while/body/eval_jaxpr/all_gather | solution.py:45
  362.3 50.0 %collective-permute-start = (bf16[512,16,128]{2,1,0:T(8,128)(2,1)}, bf16[512,16,128]{2,1,0:T(8,128)(2,1)}, u32[]{:S(2)}, u32[]{:S(2)}) collective-permute-start(bf16[512,16,128]{2,1,0:T(8,128)(2,1)} %all-gather.6.cloned.1.call-done), channel_id=1, source_target_pairs={{0,32},{32,64},{64,96},{1,33},{33,65},{65,97},{2,34},{34,66},{66,9... | collective-permute-start | bytes 6291464 | tf_op jit(solution)/shard_map/while/body/eval_jaxpr/ppermute | solution.py:10
  414.5 2.6 copy-start.2
  418.1 0.7 copy-start.4
Sparse Core Ops, SparseCore 0:
  9.6 46.3 all-gather.3
  114.9 43.2 all-gather.5
  217.1 43.2 all-gather.5
  319.0 43.2 all-gather.5
where the time goes:
time: 426 us; the launch traced here: 425 us
  waiting for transfers between devices  361 us (85%)
  local copies, waits for them, and re-layouts  17.2 us (4%)
  matrix products  16.3 us (4%)
  between operations  13.2 us (3%)
  starting transfers between devices  12.6 us (3%)
  other arithmetic  5.17 us (1%)
    ppermute x4, waiting for transfers between devices, from_behind(): return lax.ppermute(value, axis, pairs)  174 us
    all_gather x3, waiting for transfers between devices, level_turn(): gathered = lax.all_gather(outgoing, 'grp', axis=0, tiled=True)  137 us
    all_gather x1, waiting for transfers between devices, shards(): whole = lax.all_gather(own, 'grp', axis=0, tiled=True)  48.8 us
    ppermute x4, starting transfers between devices, from_behind(): return lax.ppermute(value, axis, pairs)  12.6 us
    dot_general x5, matrix products, band_term(): jnp.einsum('bkrc,bkcq->brq', pieces, tiles, preferred_element_type=jnp.fl...  12.3 us
    gather x5, local copies, waits for them, and re-layouts, band_term(): pieces = source[cols]  11.3 us
  transfers between devices with their start and end apart: 8, of which 8 were waited for; matrix products, arithmetic and copies ran while one was open for 3% of the time, Pallas kernels for 0%

commit v1 on v0

--- a/solution.py
+++ b/solution.py
@@ -42,7 +42,9 @@
 
     def level_turn(turn, current):
         outgoing = current.astype(jnp.bfloat16)
-        gathered = lax.all_gather(outgoing, "grp", axis=0, tiled=True)
+        gathered = jnp.concatenate(
+            lax.all_to_all(jnp.stack([outgoing] * lax.axis_size("grp")), "grp", 0, 0), axis=0
+        )
         panel = from_behind(gathered, "level", 1)
         resid = base - band_term(down_here, cols[:, 0], counts[:, 0], panel)
         return solve_blocks(resid, inverse)

time: 426 us -> 387 us (0.908)
  waiting for transfers between devices: 361 us -> 223 us
  blocking collectives: 0 us -> 98.2 us
    all_gather x3 -> x0, waiting for transfers between devices: 137 us -> none  [level_turn(): gathered = lax.all_gather(outgoing, 'grp', axis=0, tiled=True)]
    all_to_all x0 -> x3, blocking collectives: none -> 98.2 us  [level_turn(): lax.all_to_all(jnp.stack([outgoing] * lax.axis_size('grp')), 'grp', 0, 0)]
  transfers between devices with their start and end apart: 8 -> 5, of which waited for: 8 -> 5; matrix products, arithmetic and copies ran while one was open for 3% -> 3% of each run, Pallas kernels for 0% -> 0%
where the time goes in v1:
time: 387 us; the launch traced here: 386 us
  waiting for transfers between devices  223 us (58%)
  blocking collectives  98.2 us (25%)
  local copies, waits for them, and re-layouts  18.6 us (5%)
  matrix products  16.3 us (4%)
  between operations  13.5 us (3%)
  starting transfers between devices  12.6 us (3%)
    ppermute x4, waiting for transfers between devices, from_behind(): return lax.ppermute(value, axis, pairs)  174 us
    all_to_all x3, blocking collectives, level_turn(): lax.all_to_all(jnp.stack([outgoing] * lax.axis_size('grp')), 'grp', 0, 0)  98.2 us
    all_gather x1, waiting for transfers between devices, shards(): whole = lax.all_gather(own, 'grp', axis=0, tiled=True)  48.8 us
    ppermute x4, starting transfers between devices, from_behind(): return lax.ppermute(value, axis, pairs)  12.6 us
    dot_general x5, matrix products, band_term(): jnp.einsum('bkrc,bkcq->brq', pieces, tiles, preferred_element_type=jnp.fl...  12.3 us
    gather x5, local copies, waits for them, and re-layouts, band_term(): pieces = source[cols]  11.3 us
  transfers between devices with their start and end apart: 5, of which 5 were waited for; matrix products, arithmetic and copies ran while one was open for 3% of the time, Pallas kernels for 0%

profile of v1, /device:TPU:2, one launch (start us, length us, event | category | flops | bytes accessed | tf_op | source)
XLA Modules:
  0.0 386.1 jit_solution(2795664720138875481)
XLA Ops:
  7.3 48.8 %all-gather.3.cloned.1.call-done = bf16[1,512,16,128]{3,2,0,1:T(8,128)(2,1)} async-done(((bf16[1,16,16,128]{3,2,0,1:T(8,128)(2,1)}), bf16[1,512,16,128]{3,2,0,1:T(8,128)(2,1)}) %all-gather.3.cloned.1.call-update) | async-done | bytes 2097168 | tf_op jit(solution)/shard_map/all_gather | solution.py:33
  56.0 2.5 collective-permute-start.1
  58.5 1.3 copy.28
  59.8 0.8 compare_select_fusion.1
  62.1 2.3 gather_fusion.1
  64.4 2.1 fusion.18
  66.5 39.5 %collective-permute-done.1 = bf16[512,16,128]{2,1,0:T(8,128)(2,1)} collective-permute-done((bf16[512,16,128]{2,1,0:T(8,128)(2,1)}, bf16[512,16,128]{2,1,0:T(8,128)(2,1)}, u32[]{:S(2)}, u32[]{:S(2)}) %collective-permute-start.1) | collective-permute-done | bytes 2097184 | tf_op jit(solution)/shard_map/ppermute | solution.py:10
  106.0 2.3 gather_fusion.2
  108.3 2.5 fusion.15
  110.9 1.0 fusion.27
  111.8 266.7 %while.10 = (s32[]{:T(128)}, f32[16,16,128]{2,1,0:T(8,128)S(1)}, s32[16,3]{0,1:T(4,128)}, s32[16,3,6]{0,1,2:T(4,128)}, bf16[16,6,128,128]{3,2,1,0:T(8,128)(2,1)}...) while((s32[]{:T(128)}, f32[16,16,128]{2,1,0:T(8,128)S(1)}, s32[16,3]{0,1:T(4,128)}, ...), condition=%wide.region_1.2_spmd, body=%wide.region_0.1_spmd.sunk | while | flops 100926848 | bytes 25042456 | solution.py:52
  112.3 33.7 %all_to_all.6 = bf16[32,16,16,128]{3,2,1,0:T(8,128)(2,1)} all-to-all(bf16[32,16,16,128]{3,2,1,0:T(8,128)(2,1)S(1)} %stack.3), channel_id=1, replica_groups=mesh['level'=4,'grp'=32] {'grp'}, dimensions={0} | all-to-all | bytes 4194304 | tf_op jit(solution)/shard_map/while/body/eval_jaxpr/all_to_all | solution.py:46
  146.0 3.4 collective-permute-start
  149.4 0.7 compare_select_fusion.4
  151.1 44.8 %collective-permute-done = bf16[512,16,128]{2,1,0:T(8,128)(2,1)} collective-permute-done((bf16[512,16,128]{2,1,0:T(8,128)(2,1)}, bf16[512,16,128]{2,1,0:T(8,128)(2,1)}, u32[]{:S(2)}, u32[]{:S(2)}) %collective-permute-start) | collective-permute-done | bytes 2097184 | tf_op jit(solution)/shard_map/while/body/eval_jaxpr/ppermute | solution.py:10
  195.9 2.3 gather_fusion
  198.2 2.5 fusion.46
  200.7 1.0 fusion.47
  202.2 32.3 %all_to_all.6 = bf16[32,16,16,128]{3,2,1,0:T(8,128)(2,1)} all-to-all(bf16[32,16,16,128]{3,2,1,0:T(8,128)(2,1)S(1)} %stack.3), channel_id=1, replica_groups=mesh['level'=4,'grp'=32] {'grp'}, dimensions={0} | all-to-all | bytes 4194304 | tf_op jit(solution)/shard_map/while/body/eval_jaxpr/all_to_all | solution.py:46
  234.5 3.4 collective-permute-start
  237.8 0.7 compare_select_fusion.4
  239.5 44.8 %collective-permute-done = bf16[512,16,128]{2,1,0:T(8,128)(2,1)} collective-permute-done((bf16[512,16,128]{2,1,0:T(8,128)(2,1)}, bf16[512,16,128]{2,1,0:T(8,128)(2,1)}, u32[]{:S(2)}, u32[]{:S(2)}) %collective-permute-start) | collective-permute-done | bytes 2097184 | tf_op jit(solution)/shard_map/while/body/eval_jaxpr/ppermute | solution.py:10
  284.3 2.3 gather_fusion
  286.6 2.5 fusion.46
  289.2 1.0 fusion.47
  290.6 32.3 %all_to_all.6 = bf16[32,16,16,128]{3,2,1,0:T(8,128)(2,1)} all-to-all(bf16[32,16,16,128]{3,2,1,0:T(8,128)(2,1)S(1)} %stack.3), channel_id=1, replica_groups=mesh['level'=4,'grp'=32] {'grp'}, dimensions={0} | all-to-all | bytes 4194304 | tf_op jit(solution)/shard_map/while/body/eval_jaxpr/all_to_all | solution.py:46
  322.9 3.4 collective-permute-start
  326.3 0.7 compare_select_fusion.4
  327.9 44.8 %collective-permute-done = bf16[512,16,128]{2,1,0:T(8,128)(2,1)} collective-permute-done((bf16[512,16,128]{2,1,0:T(8,128)(2,1)}, bf16[512,16,128]{2,1,0:T(8,128)(2,1)}, u32[]{:S(2)}, u32[]{:S(2)}) %collective-permute-start) | collective-permute-done | bytes 2097184 | tf_op jit(solution)/shard_map/while/body/eval_jaxpr/ppermute | solution.py:10
  372.7 2.3 gather_fusion
  375.0 2.5 fusion.46
  377.6 1.0 fusion.47
  (48 shorter events, 7.1 us)
Async XLA Ops:
  6.5 57.8 %copy-start = (bf16[1,16,6,128,128]{4,3,2,1,0:T(8,128)(2,1)S(1)}, bf16[1,16,6,128,128]{4,3,2,1,0:T(8,128)(2,1)}, u32[]{:S(2)}) copy-start(bf16[1,16,6,128,128]{4,3,2,1,0:T(8,128)(2,1)} %param.13) | copy-start | bytes 9437188
  6.5 49.5 %all-gather.3.cloned.1.call-start = ((), (), s32[]{:S(2)}) async-start(), calls=%async_computation.1 | async-start | bytes 2162688 | tf_op jit(solution)/shard_map/all_gather | solution.py:33
  56.0 50.0 %collective-permute-start.1 = (bf16[512,16,128]{2,1,0:T(8,128)(2,1)}, bf16[512,16,128]{2,1,0:T(8,128)(2,1)}, u32[]{:S(2)}, u32[]{:S(2)}) collective-permute-start(bf16[512,16,128]{2,1,0:T(8,128)(2,1)} %bitcast.95), channel_id=1, source_target_pairs={{32,0},{64,32},{96,64},{33,1},{65,33},{97,65},{34,2},{66,34},{98,6... | collective-permute-start | bytes 6291464 | tf_op jit(solution)/shard_map/ppermute | solution.py:10
  61.4 0.6 copy-start.5
  108.3 2.6 copy-start.1
  110.8 1.0 copy-start.3
  146.0 49.8 %collective-permute-start = (bf16[512,16,128]{2,1,0:T(8,128)(2,1)}, bf16[512,16,128]{2,1,0:T(8,128)(2,1)}, u32[]{:S(2)}, u32[]{:S(2)}) collective-permute-start(bf16[512,16,128]{2,1,0:T(8,128)(2,1)} %bitcast.88), channel_id=1, source_target_pairs={{0,32},{32,64},{64,96},{1,33},{33,65},{65,97},{2,34},{34,66},{66,9... | collective-permute-start | bytes 6291464 | tf_op jit(solution)/shard_map/while/body/eval_jaxpr/ppermute | solution.py:10
  198.2 2.6 copy-start.2
  234.5 49.8 %collective-permute-start = (bf16[512,16,128]{2,1,0:T(8,128)(2,1)}, bf16[512,16,128]{2,1,0:T(8,128)(2,1)}, u32[]{:S(2)}, u32[]{:S(2)}) collective-permute-start(bf16[512,16,128]{2,1,0:T(8,128)(2,1)} %bitcast.88), channel_id=1, source_target_pairs={{0,32},{32,64},{64,96},{1,33},{33,65},{65,97},{2,34},{34,66},{66,9... | collective-permute-start | bytes 6291464 | tf_op jit(solution)/shard_map/while/body/eval_jaxpr/ppermute | solution.py:10
  286.6 2.6 copy-start.2
  322.9 49.8 %collective-permute-start = (bf16[512,16,128]{2,1,0:T(8,128)(2,1)}, bf16[512,16,128]{2,1,0:T(8,128)(2,1)}, u32[]{:S(2)}, u32[]{:S(2)}) collective-permute-start(bf16[512,16,128]{2,1,0:T(8,128)(2,1)} %bitcast.88), channel_id=1, source_target_pairs={{0,32},{32,64},{64,96},{1,33},{33,65},{65,97},{2,34},{34,66},{66,9... | collective-permute-start | bytes 6291464 | tf_op jit(solution)/shard_map/while/body/eval_jaxpr/ppermute | solution.py:10
  375.0 2.6 copy-start.2
  378.6 0.7 copy-start.4
Sparse Core Ops, SparseCore 0:
  9.6 46.3 all-gather.2
